TPU v7x, 512 devices: a whole 4x8x8 slice. The times are simulated.
512 devices in a mesh: users: 16 (over y_lo, x), items: 32 (over z, y_hi, core).
Axes of the slice: x: 4, y: 8 (y_hi: 2, y_lo: 4; y = y_hi * 4 + y_lo), z: 8, core: 2. Of those that a mesh axis runs over, the one named last changes fastest.
Arguments:
- histories: int32 [16, 256], replicated, may hold values from 0 to 1048575
- item_degree: int32 [1048576], P('items'), may hold values from 1 to 63
- user_degree: int32 [131072], P('users'), may hold values from 1 to 63
- tile_values: float32 [16, 32, 24, 128, 128], P('users', 'items'), may hold values from 0 to 1
- tile_rows: int32 [16, 32, 24], P('users', 'items'), may hold values from 0 to 63
- tile_cols: int32 [16, 32, 24], P('users', 'items'), may hold values from 0 to 255
- tile_count: int32 [16, 32], P('users', 'items'), may hold values from 1 to 24, as said below
Outputs:
- scores: float32 [16, 1048576], P('users', 'items')
Inputs may be any that keep to these rules, and one draw needn't show every extreme that they name: `tile_count`: every device has 1 to 24 live slots, and some device has exactly 24.
All inputs are finite; a program needn't handle non-finite values.
Results may differ from a plain program's by a relative error of at most 0.0003.
Values sent between devices are 32-bit elements; how exact they have to be, the bound alone decides.
A program may use at most 64 MiB of HBM per device.

v0:
```python
import jax
import jax.numpy as jnp
from jax import lax
from jax.sharding import PartitionSpec as P


def body(histories, item_degree, user_degree, tile_values, tile_rows, tile_cols, tile_count):
    highest = lax.Precision.HIGHEST
    queries = histories.shape[0]
    items_local = item_degree.shape[0]
    users_local = user_degree.shape[0]
    width = tile_values.shape[-1]
    item_blocks = items_local // width
    user_blocks = users_local // width
    values_now = tile_values[0, 0]
    block_rows = tile_rows[0, 0]
    block_cols = tile_cols[0, 0]
    slot_ids = jnp.arange(values_now.shape[0], dtype=jnp.int32)
    alive_mask = (slot_ids < tile_count[0, 0]).astype(jnp.float32)
    offset = lax.axis_index("items") * items_local
    local_ids = histories - offset
    inside = (local_ids >= 0) & (local_ids < items_local)
    query_ids = jnp.broadcast_to(jnp.arange(queries, dtype=jnp.int32)[:, None], histories.shape)
    hits = (
        jnp.zeros((queries, items_local), jnp.float32)
        .at[query_ids, jnp.clip(local_ids, 0, items_local - 1)]
        .add(jnp.where(inside, 1.0, 0.0))
    )
    item_scale = lax.rsqrt(item_degree.astype(jnp.float32))
    panels = (hits * item_scale[None, :]).reshape(queries, item_blocks, width)
    picked = jnp.take(panels, block_cols, axis=1)
    partial_value = jnp.einsum("qtk,tjk->qtj", picked, values_now, precision=highest)
    row_onehot = (block_rows[:, None] == jnp.arange(user_blocks, dtype=jnp.int32)[None, :]).astype(
        jnp.float32
    ) * alive_mask[:, None]
    user_terms = jnp.einsum("qtj,tu->quj", partial_value, row_onehot, precision=highest)
    user_scale = (1.0 / user_degree.astype(jnp.float32)).reshape(user_blocks, width)
    user_totals = lax.psum(user_terms, "items")
    weighted = user_totals * user_scale[None, :, :]
    picked_users = jnp.take(weighted, block_rows, axis=1)
    score_part = jnp.einsum("qtj,tjk->qtk", picked_users, values_now, precision=highest)
    block_range = jnp.arange(item_blocks, dtype=jnp.int32)
    col_onehot = (block_cols[:, None] == block_range[None, :]).astype(jnp.float32) * alive_mask[
        :, None
    ]
    score_terms = jnp.einsum("qtk,tb->qbk", score_part, col_onehot, precision=highest).reshape(
        queries, items_local
    )
    score_totals = lax.psum(score_terms, "users")
    count = queries // lax.axis_size("users")
    score_rows = lax.dynamic_slice_in_dim(score_totals, lax.axis_index("users") * count, count, 0)
    return score_rows * item_scale[None, :]


def solution(mesh):
    in_specs = (
        P(),
        P("items"),
        P("users"),
        P("users", "items", None, None, None),
        P("users", "items", None),
        P("users", "items", None),
        P("users", "items"),
    )
    out_specs = P("users", "items")
    return jax.shard_map(body, mesh=mesh, in_specs=in_specs, out_specs=out_specs, check_vma=False)
```

profile of v0, /device:TPU:2, one launch (start us, length us, event | category | flops | bytes accessed | tf_op | source)
XLA Modules:
  0.0 588.5 jit_solution(13323144484975118217)
XLA Ops:
  6.5 0.0 copy-start
  6.5 0.0 all-reduce.3.cloned.1.call-start
  6.5 0.8 fusion.25
  7.4 0.7 select_bitcast_fusion.1
  8.1 0.7 fusion.34
  8.8 0.7 compare_and_fusion
  9.4 0.7 multiply_reduce_fusion
  10.2 0.7 and_reduce_fusion
  10.9 29.4 %scatter_custom_fusion = f32[524288]{0:T(1024)} fusion(s32[4096]{0:T(1024)S(1)} %bitcast.65, f32[4096]{0:T(1024)S(1)} %bitcast.66, f32[]{:T(128)} %constant.18.clone.1), kind=kCustom, calls=%fused_computation.13 | custom fusion | flops 4096 | bytes 2097156
  40.3 2.8 reshape.100
  43.1 0.0 copy-done.1
  43.8 3.1 copy_bitcast_fusion.1
  46.9 2.2 gather_fusion
  49.1 0.0 copy-done
  49.1 2.6 fusion.4
  51.7 0.0 copy-done.3
  51.7 1.5 convolution_bitcast_fusion
  53.2 0.0 all-reduce.3.cloned.1.call-update
  53.2 0.0 all-reduce.5.cloned.1.call-start
  53.3 0.0 copy-done.2
  53.4 0.0 copy-start.4
  53.4 347.5 %all-reduce.3.cloned.1.call-done = f32[16,64,128]{2,1,0:T(8,128)} async-done(((f32[16,64,128]{2,1,0:T(8,128)}), f32[16,64,128]{2,1,0:T(8,128)}) %all-reduce.3.cloned.1.call-update) | async-done | bytes 524304 | tf_op jit(solution)/shard_map/psum | solution.py:38
  400.9 1.1 broadcast_multiply_fusion
  402.0 0.3 copy.16
  402.3 0.6 gather_fusion.1
  402.9 1.5 fusion.7
  404.4 0.0 copy-done.4
  404.4 1.9 fusion.14
  406.3 2.5 copy.28
  408.8 0.0 all-reduce.5.cloned.1.call-update
  408.8 170.8 %all-reduce.5.cloned.1.call-done = f32[16,32768]{1,0:T(8,128)} async-done(((f32[16,32768]{1,0:T(8,128)}), f32[16,32768]{1,0:T(8,128)}) %all-reduce.5.cloned.1.call-update) | async-done | bytes 2097168 | tf_op jit(solution)/shard_map/psum | solution.py:49
  579.7 2.0 dynamic-slice_multiply_fusion
  (14 shorter events, 0.1 us)
Async XLA Ops:
  6.5 42.6 %copy-start = (f32[1,1,24,128,128]{4,3,2,1,0:T(8,128)S(1)}, f32[1,1,24,128,128]{4,3,2,1,0:T(8,128)}, u32[]{:S(2)}) copy-start(f32[1,1,24,128,128]{4,3,2,1,0:T(8,128)} %param.10) | copy-start | bytes 4718596
  6.5 394.4 %all-reduce.3.cloned.1.call-start = ((), (), s32[]{:S(2)}) async-start(), calls=%async_computation | async-start | bytes 1048576 | tf_op jit(solution)/shard_map/psum | solution.py:38
  40.3 2.8 copy-start.1
  46.9 4.8 copy-start.3
  46.9 6.4 %copy-start.2 = (s32[8192]{0:T(1024)S(1)}, s32[8192]{0:T(1024)}, u32[]{:S(2)}) copy-start(s32[8192]{0:T(1024)} %param.9) | copy-start | bytes 98308
  53.2 526.4 %all-reduce.5.cloned.1.call-start = ((), (), s32[]{:S(2)}) async-start(), calls=%async_computation.1 | async-start | bytes 4194304 | tf_op jit(solution)/shard_map/psum | solution.py:49
  53.4 351.0 %copy-start.4 = (s32[1,1,24]{2,1,0:T(1,128)S(1)}, s32[1,1,24]{2,1,0:T(1,128)}, u32[]{:S(2)}) copy-start(s32[1,1,24]{2,1,0:T(1,128)} %param.12) | copy-start | bytes 292
Sparse Core Ops, SparseCore 0:
  53.4 347.4 all-reduce.2
  409.0 170.6 all-reduce.4
where the time goes:
time: 589 us
  waiting for transfers between devices  518 us (88%)
  other arithmetic  40 us (7%)
  between operations  14.2 us (2%)
  local copies, waits for them, and re-layouts  8.42 us (1%)
  matrix products  7.49 us (1%)
    psum x1, waiting for transfers between devices, body(): user_totals = lax.psum(user_terms, 'items')  348 us
    psum x1, waiting for transfers between devices, body(): score_totals = lax.psum(score_terms, 'users')  171 us
    unnamed x5, other arithmetic  31.6 us
  transfers between devices with their start and end apart: 2, of which 2 were waited for; matrix products, arithmetic and copies ran while one was open for 0% of the time, Pallas kernels for 0%

commit v1 on v0

--- a/solution.py
+++ b/solution.py
@@ -35,7 +35,7 @@
     ) * alive_mask[:, None]
     user_terms = jnp.einsum("qtj,tu->quj", partial_value, row_onehot, precision=highest)
     user_scale = (1.0 / user_degree.astype(jnp.float32)).reshape(user_blocks, width)
-    user_totals = lax.psum(user_terms, "items")
+    user_totals = jnp.sum(lax.all_gather(user_terms, "items"), axis=0)
     weighted = user_totals * user_scale[None, :, :]
     picked_users = jnp.take(weighted, block_rows, axis=1)
     score_part = jnp.einsum("qtj,tjk->qtk", picked_users, values_now, precision=highest)

time: 589 us -> 444 us (0.75)
  waiting for transfers between devices: 518 us -> 368 us
  other arithmetic: 40 us -> 46.7 us
    psum x1 -> x0, waiting for transfers between devices: 348 us -> none  [body(): user_totals = lax.psum(user_terms, 'items')]
    all_gather x0 -> x1, waiting for transfers between devices: none -> 200 us  [body(): user_totals = jnp.sum(lax.all_gather(user_terms, 'items'), axis=0)]
    reduce_sum x0 -> x1, other arithmetic: none -> 7.45 us  [body(): user_totals = jnp.sum(lax.all_gather(user_terms, 'items'), axis=0)]
where the time goes in v1:
time: 444 us
  waiting for transfers between devices  368 us (83%)
  other arithmetic  46.7 us (11%)
  between operations  14.2 us (3%)
  local copies, waits for them, and re-layouts  8.11 us (2%)
  matrix products  7.46 us (2%)
    all_gather x1, waiting for transfers between devices, body(): user_totals = jnp.sum(lax.all_gather(user_terms, 'items'), axis=0)  200 us
    psum x1, waiting for transfers between devices, body(): score_totals = lax.psum(score_terms, 'users')  168 us
    unnamed x5, other arithmetic  31.6 us
  transfers between devices with their start and end apart: 2, of which 2 were waited for; matrix products, arithmetic and copies ran while one was open for 0% of the time, Pallas kernels for 0%

profile of v1, /device:TPU:2, one launch (start us, length us, event | category | flops | bytes accessed | tf_op | source)
XLA Modules:
  0.0 444.1 jit_solution(17921575302995927580)
XLA Ops:
  6.5 0.0 copy-start
  6.5 0.0 all-gather.3.cloned.1.call-start
  6.5 0.8 fusion.25
  7.4 0.7 select_bitcast_fusion.1
  8.1 0.7 fusion.34
  8.8 0.7 compare_and_fusion
  9.4 0.7 multiply_reduce_fusion
  10.2 0.7 and_reduce_fusion
  10.9 29.4 %scatter_custom_fusion = f32[524288]{0:T(1024)} fusion(s32[4096]{0:T(1024)S(1)} %bitcast.67, f32[4096]{0:T(1024)S(1)} %bitcast.68, f32[]{:T(128)} %constant.18.clone.1), kind=kCustom, calls=%fused_computation.13 | custom fusion | flops 4096 | bytes 2097156
  40.3 2.8 reshape.100
  43.1 0.0 copy-done.1
  43.8 3.1 copy_bitcast_fusion.1
  46.9 2.2 gather_fusion
  49.1 0.0 copy-done
  49.1 2.6 fusion.4
  51.7 0.0 copy-done.3
  51.7 1.5 convolution_bitcast_fusion
  53.2 0.0 all-gather.3.cloned.1.call-update
  53.2 0.0 all-reduce.2.cloned.1.call-start
  53.3 0.0 copy-done.2
  53.4 199.8 %all-gather.3.cloned.1.call-done = f32[512,64,128]{2,1,0:T(8,128)} async-done(((f32[16,64,128]{2,1,0:T(8,128)}), f32[512,64,128]{2,1,0:T(8,128)}) %all-gather.3.cloned.1.call-update) | async-done | bytes 16777232 | tf_op jit(solution)/shard_map/all_gather | solution.py:38
  253.2 7.5 %reduce_sum.9 = f32[16,64,128]{2,1,0:T(8,128)S(1)} reduce(f32[32,16,64,128]{3,2,1,0:T(8,128)} %bitcast.63, f32[]{:T(128)} %constant.18.clone.1), dimensions={0}, to_apply=%region_1.2 | reduce | flops 4063232 | bytes 17301508 | tf_op jit(solution)/shard_map/reduce_sum | solution.py:38
  260.6 0.0 copy-start.4
  260.7 0.3 copy_multiply_fusion
  261.0 0.6 gather_fusion.1
  261.6 1.5 fusion.7
  263.0 0.0 copy-done.4
  263.1 1.9 fusion.14
  265.0 2.5 copy.26
  267.5 0.0 all-reduce.2.cloned.1.call-update
  267.5 167.7 %all-reduce.2.cloned.1.call-done = f32[16,32768]{1,0:T(8,128)} async-done(((f32[16,32768]{1,0:T(8,128)}), f32[16,32768]{1,0:T(8,128)}) %all-reduce.2.cloned.1.call-update) | async-done | bytes 2097168 | tf_op jit(solution)/shard_map/psum | solution.py:49
  435.2 2.0 dynamic-slice_multiply_fusion
  (14 shorter events, 0.1 us)
Async XLA Ops:
  6.5 42.6 %copy-start = (f32[1,1,24,128,128]{4,3,2,1,0:T(8,128)S(1)}, f32[1,1,24,128,128]{4,3,2,1,0:T(8,128)}, u32[]{:S(2)}) copy-start(f32[1,1,24,128,128]{4,3,2,1,0:T(8,128)} %param.10) | copy-start | bytes 4718596
  6.5 246.6 %all-gather.3.cloned.1.call-start = ((), (), s32[]{:S(2)}) async-start(), calls=%async_computation.1 | async-start | bytes 17301504 | tf_op jit(solution)/shard_map/all_gather | solution.py:38
  40.3 2.8 copy-start.1
  46.9 4.8 %copy-start.3 = (s32[1,1,24]{2,1,0:T(1,128)S(1)}, s32[1,1,24]{2,1,0:T(1,128)}, u32[]{:S(2)}) copy-start(s32[1,1,24]{2,1,0:T(1,128)} %param.11) | copy-start | bytes 292
  46.9 6.4 %copy-start.2 = (s32[8192]{0:T(1024)S(1)}, s32[8192]{0:T(1024)}, u32[]{:S(2)}) copy-start(s32[8192]{0:T(1024)} %param.9) | copy-start | bytes 98308
  53.2 382.0 %all-reduce.2.cloned.1.call-start = ((), (), s32[]{:S(2)}) async-start(), calls=%async_computation | async-start | bytes 4194304 | tf_op jit(solution)/shard_map/psum | solution.py:49
  260.6 2.4 copy-start.4
Sparse Core Ops, SparseCore 0:
  53.4 199.7 all-gather.2
  267.6 167.5 all-reduce.1
